TPU v7x, 32 devices: a whole 2x2x4 slice. The times are simulated.
32 devices in a mesh: fsdp: 4 (over x, core), ctx: 4 (over z), ch: 2 (over y).
Axes of the slice: x: 2, y: 2, z: 4, core: 2. Of those that a mesh axis runs over, the one named last changes fastest.
Arguments:
- tokens: bfloat16 [4096, 4096], P(('fsdp', 'ctx'), 'ch'), may hold values from -6 to 6
- w_query: bfloat16 [4096, 2048], P(('fsdp', 'ctx'), 'ch'), may hold values from -0.09375 to 0.09375
- w_key: bfloat16 [4096, 2048], P(('fsdp', 'ctx'), 'ch'), may hold values from -0.09375 to 0.09375
- w_value: bfloat16 [4096, 2048], P(('fsdp', 'ctx'), 'ch'), may hold values from -0.09375 to 0.09375
- short_taps: float32 [3, 3, 2048], P(None, None, 'ch'), may hold values from -3 to 3
- long_filter: float32 [4096, 2048], P(('fsdp', 'ctx'), 'ch'), may hold values from -6 to 6
- filter_bias: float32 [2048], P('ch'), may hold values from -4 to 4
Outputs:
- mixed_out: bfloat16 [4096, 2048], P(('fsdp', 'ctx'), 'ch')
All inputs are finite; a program needn't handle non-finite values.
Results may differ from a plain program's by a relative error of at most 0.0064.
Values may be sent and summed in bfloat16 or wider, within the bound.
No kernel may reach another device: no remote copies, remote signals or barrier semaphores. Data moves between devices by JAX's collectives and lax.ppermute only.
A program may use at most 128 MiB of HBM per device.

v0:
```python
import math

import jax
import jax.numpy as jnp
from jax import lax
from jax.sharding import PartitionSpec as P

HIGHEST = lax.Precision.HIGHEST


def shifted(x, axis, by):
    size = lax.axis_size(axis)
    pairs = [(i, i + by) for i in range(size) if 0 <= i + by < size]
    return lax.ppermute(x, axis, pairs)


def phase_table(product, modulus):
    angles = 2.0 * math.pi / modulus * (product % modulus).astype(jnp.float32)
    return (jnp.cos(angles), jnp.sin(angles))


def regroup(stacked):
    return lax.all_to_all(stacked, ("fsdp", "ctx"), split_axis=1, concat_axis=1, tiled=True)


def add_three(gathered):

    def fold_rows(totals, pieces, start):
        return (
            jnp.dot(gathered, pieces[0], preferred_element_type=jnp.float32),
            jnp.dot(gathered, pieces[1], preferred_element_type=jnp.float32),
            jnp.dot(gathered, pieces[2], preferred_element_type=jnp.float32),
        )

    return fold_rows


def spread_conv(gated, long_filter):
    row_count, channels = gated.shape
    blocks = lax.axis_size(("fsdp", "ctx"))
    groups = row_count // blocks
    total_len = 2 * blocks * row_count
    device = lax.axis_index(("fsdp", "ctx"))
    half_idx = jnp.arange(2, dtype=jnp.int32)
    block_idx = jnp.arange(blocks, dtype=jnp.int32)
    group_idx = jnp.arange(groups, dtype=jnp.int32)
    row_idx = jnp.arange(row_count, dtype=jnp.int32)
    coarse = 2 * block_idx[None, :] + half_idx[:, None]
    cos_block, sin_block = phase_table(coarse[:, :, None] * block_idx[None, None, :], 2 * blocks)
    fine_fwd = device * groups + group_idx
    cos_twist, sin_twist = phase_table(coarse[:, :, None] * fine_fwd[None, None, :], total_len)
    cos_row, sin_row = phase_table(row_idx[:, None] * row_idx[None, :], row_count)
    own_coarse = 2 * device + half_idx
    cos_back, sin_back = phase_table(own_coarse[:, None] * row_idx[None, :], total_len)
    received = regroup(jnp.stack([gated, long_filter]).reshape(2, blocks, groups, channels))
    real_coarse = jnp.einsum("sjn,bngc->bsjgc", cos_block, received, precision=HIGHEST)
    imag_coarse = -jnp.einsum("sjn,bngc->bsjgc", sin_block, received, precision=HIGHEST)
    twist_cos = cos_twist[None, :, :, :, None]
    twist_sin = sin_twist[None, :, :, :, None]
    real_twist = real_coarse * twist_cos + imag_coarse * twist_sin
    imag_twist = imag_coarse * twist_cos - real_coarse * twist_sin
    packed = jnp.stack([real_twist, imag_twist], axis=1).reshape(8, blocks, groups, channels)
    spread = regroup(packed).reshape(2, 2, 2, row_count, channels)
    spec_re = jnp.einsum("kn,bsnc->bskc", cos_row, spread[:, 0], precision=HIGHEST) + jnp.einsum(
        "kn,bsnc->bskc", sin_row, spread[:, 1], precision=HIGHEST
    )
    spec_im = jnp.einsum("kn,bsnc->bskc", cos_row, spread[:, 1], precision=HIGHEST) - jnp.einsum(
        "kn,bsnc->bskc", sin_row, spread[:, 0], precision=HIGHEST
    )
    prod_re = spec_re[0] * spec_re[1] - spec_im[0] * spec_im[1]
    prod_im = spec_re[0] * spec_im[1] + spec_im[0] * spec_re[1]
    back_re = jnp.einsum("nk,skc->snc", cos_row, prod_re, precision=HIGHEST) - jnp.einsum(
        "nk,skc->snc", sin_row, prod_im, precision=HIGHEST
    )
    back_im = jnp.einsum("nk,skc->snc", cos_row, prod_im, precision=HIGHEST) + jnp.einsum(
        "nk,skc->snc", sin_row, prod_re, precision=HIGHEST
    )
    untwist_cos = cos_back[:, :, None]
    untwist_sin = sin_back[:, :, None]
    real_untwist = back_re * untwist_cos - back_im * untwist_sin
    imag_untwist = back_re * untwist_sin + back_im * untwist_cos
    returned = jnp.stack([real_untwist, imag_untwist]).reshape(4, blocks, groups, channels)
    coarse_back = regroup(returned).reshape(2, 2, blocks, groups, channels)
    outputs = (
        jnp.einsum("sjn,sjgc->ngc", cos_block, coarse_back[0], precision=HIGHEST)
        - jnp.einsum("sjn,sjgc->ngc", sin_block, coarse_back[1], precision=HIGHEST)
    ) / total_len
    return regroup(outputs[None]).reshape(row_count, channels)


def on_device(tokens, w_query, w_key, w_value, short_taps, long_filter, filter_bias):
    gathered = lax.all_gather(tokens, "ch", axis=1, tiled=True)
    row_count = gathered.shape[0]
    channels = w_query.shape[1]
    zeros_init = jnp.zeros((row_count, channels), jnp.float32)
    fold_rows = add_three(gathered)
    totals = fold_rows(
        (zeros_init, zeros_init, zeros_init),
        (
            lax.all_gather(w_query, ("fsdp", "ctx"), axis=0, tiled=True),
            lax.all_gather(w_key, ("fsdp", "ctx"), axis=0, tiled=True),
            lax.all_gather(w_value, ("fsdp", "ctx"), axis=0, tiled=True),
        ),
        jnp.int32(0),
    )
    streams = jnp.stack([totals[0], totals[1], totals[2]]).astype(jnp.bfloat16)
    tails = streams[:, row_count - 2 :, :]
    earlier = shifted(tails, ("fsdp", "ctx"), 1)
    extended = jnp.concatenate([earlier, streams], axis=1).astype(jnp.float32)
    filtered = (
        short_taps[:, 0:1, :] * extended[:, 2:, :]
        + short_taps[:, 1:2, :] * extended[:, 1:-1, :]
        + short_taps[:, 2:3, :] * extended[:, :-2, :]
    )
    query_conv = filtered[0]
    gated = filtered[1] * filtered[2]
    conv = spread_conv(gated, long_filter)
    return (query_conv * (conv + filter_bias[None, :] * gated)).astype(jnp.bfloat16)


def solution(mesh):
    return jax.shard_map(
        on_device,
        mesh=mesh,
        in_specs=(
            P(("fsdp", "ctx"), "ch"),
            P(("fsdp", "ctx"), "ch"),
            P(("fsdp", "ctx"), "ch"),
            P(("fsdp", "ctx"), "ch"),
            P(None, None, "ch"),
            P(("fsdp", "ctx"), "ch"),
            P("ch"),
        ),
        out_specs=P(("fsdp", "ctx"), "ch"),
        check_vma=False,
    )
```

profile of v0, /device:TPU:0, one launch (start us, length us, event | category | flops | bytes accessed | tf_op | source)
XLA Modules:
  0.0 765.6 jit_solution(9050508467287578637)
XLA Ops:
  10.3 34.5 %all-gather.5.cloned.1.call-done = bf16[256,4096]{1,0:T(8,128)(2,1)} async-done(((bf16[256,2048]{1,0:T(8,128)(2,1)}), bf16[256,4096]{1,0:T(8,128)(2,1)}) %all-gather.5.cloned.1.call-update) | async-done | bytes 2097168 | tf_op jit(solution)/shard_map/all_gather | solution.py:92
  44.8 77.1 %all-gather.7.cloned.1.call-done = bf16[4096,1024]{1,0:T(8,128)(2,1)} async-done(((bf16[256,1024]{1,0:T(8,128)(2,1)}), bf16[4096,1024]{1,0:T(8,128)(2,1)}) %all-gather.7.cloned.1.call-update) | async-done | bytes 8388624 | tf_op jit(solution)/shard_map/all_gather | solution.py:100
  121.9 6.3 fusion.47
  128.2 69.0 %all-gather.9.cloned.1.call-done = bf16[4096,1024]{1,0:T(8,128)(2,1)} async-done(((bf16[256,1024]{1,0:T(8,128)(2,1)}), bf16[4096,1024]{1,0:T(8,128)(2,1)}) %all-gather.9.cloned.1.call-update) | async-done | bytes 8388624 | tf_op jit(solution)/shard_map/all_gather | solution.py:101
  197.3 5.8 fusion.48
  203.1 69.5 %all-gather.11.cloned.1.call-done = bf16[4096,1024]{1,0:T(8,128)(2,1)} async-done(((bf16[256,1024]{1,0:T(8,128)(2,1)}), bf16[4096,1024]{1,0:T(8,128)(2,1)}) %all-gather.11.cloned.1.call-update) | async-done | bytes 8388624 | tf_op jit(solution)/shard_map/all_gather | solution.py:102
  272.5 5.8 fusion.49
  287.7 5.7 all-to-all-start
  293.6 48.9 %all-to-all-done = f32[2,16,16,1024]{3,2,0,1:T(8,128)S(1)} async-done(((f32[2,16,16,1024]{3,2,0,1:T(8,128)}), f32[2,16,16,1024]{3,2,0,1:T(8,128)S(1)}, u32[]{:S(2)}, u32[]{:S(2)}) %all-to-all-start) | async-done | bytes 2097184 | tf_op jit(solution)/shard_map/all_to_all | solution.py:23
  342.6 6.2 fusion.22
  348.7 7.4 fusion.1
  357.8 17.4 %copy.41 = f32[2,2,2,16,16,1024]{5,4,3,2,1,0:T(8,128)S(1)} copy(f32[2,2,2,16,16,1024]{5,3,2,4,0,1:T(8,128)S(1)} %pad_maximum_fusion) | data formatting | bytes 16777216 | tf_op jit(solution)/shard_map/stack | solution.py:62
  375.2 4.1 copy.42
  379.3 4.8 all-to-all-start.1
  384.2 184.1 %all-to-all-done.1 = f32[8,16,16,1024]{3,2,0,1:T(8,128)} async-done(((f32[8,16,16,1024]{3,2,0,1:T(8,128)}), f32[8,16,16,1024]{3,2,0,1:T(8,128)}, u32[]{:S(2)}, u32[]{:S(2)}) %all-to-all-start.1) | async-done | bytes 8388640 | tf_op jit(solution)/shard_map/all_to_all | solution.py:23
  568.3 4.2 copy.43
  572.5 8.0 %fusion.5 = f32[2,2,1024,256]{3,2,1,0:T(8,128)S(1)} fusion(f32[2,2,2,256,1024]{4,3,2,1,0:T(8,128)S(1)} %bitcast.160), kind=kOutput, calls=%fused_computation.15 | convolution fusion | flops 3222142976 | bytes 8388608 | tf_op jit(solution)/shard_map/kn,bsnc->bskc/dot_general | solution.py:64
  580.5 8.4 %fusion.4 = f32[2,2,1024,256]{3,2,1,0:T(8,128)S(1)} fusion(f32[2,2,2,256,1024]{4,3,2,1,0:T(8,128)S(1)} %bitcast.161), kind=kOutput, calls=%fused_computation.14 | convolution fusion | flops 3222142976 | bytes 8388608 | tf_op jit(solution)/shard_map/kn,bsnc->bskc/dot_general | solution.py:67
  588.9 8.2 %add_bitcast_fusion = f32[2,2,256,1024]{2,3,1,0:T(8,128)S(1)} fusion(f32[2,2,1024,256]{3,2,1,0:T(8,128)S(1)} %fusion.5, f32[2,2,2,256,1024]{4,3,2,1,0:T(8,128)S(1)} %bitcast.162), kind=kOutput, calls=%fused_computation.13 | convolution fusion | flops 3223191552 | bytes 12582912 | tf_op jit(solution)/shard_map/kn,bsnc->bskc/dot_general | solution.py:64
  597.1 8.2 %subtract_bitcast_fusion = f32[2,2,256,1024]{2,3,1,0:T(8,128)S(1)} fusion(f32[2,2,1024,256]{3,2,1,0:T(8,128)S(1)} %fusion.4, f32[2,2,2,256,1024]{4,3,2,1,0:T(8,128)S(1)} %bitcast.163), kind=kOutput, calls=%fused_computation.12 | convolution fusion | flops 3223191552 | bytes 12582912 | tf_op jit(solution)/shard_map/kn,bsnc->bskc/dot_general | solution.py:67
  608.8 3.2 fusion.14
  615.1 3.5 subtract_bitcast_fusion.1
  622.0 97.6 %all_to_all.20 = f32[4,16,16,1024]{3,0,2,1:T(4,128)S(1)} all-to-all(f32[4,16,16,1024]{3,0,2,1:T(4,128)S(1)} %copy.50), channel_id=1, replica_groups=mesh['fsdp'=4,'ctx'=4,'ch'=2] {'fsdp','ctx'}, dimensions={1} | all-to-all | bytes 8388608 | tf_op jit(solution)/shard_map/all_to_all | solution.py:23
  727.1 30.2 %all_to_all.21 = f32[1,16,16,1024]{3,2,0,1:T(8,128)S(1)} all-to-all(f32[1,16,16,1024]{3,2,0,1:T(8,128)S(1)} %copy.53), channel_id=1, replica_groups=mesh['fsdp'=4,'ctx'=4,'ch'=2] {'fsdp','ctx'}, dimensions={1} | all-to-all | bytes 2097152 | tf_op jit(solution)/shard_map/all_to_all | solution.py:23
  (48 shorter events, 33.7 us)
Async XLA Ops:
  6.5 38.2 %all-gather.5.cloned.1.call-start = ((), (), s32[]{:S(2)}) async-start(), calls=%async_computation.4 | async-start | bytes 3145728 | tf_op jit(solution)/shard_map/all_gather | solution.py:92
  7.3 114.6 %all-gather.7.cloned.1.call-start = ((), (), s32[]{:S(2)}) async-start(), calls=%async_computation.5 | async-start | bytes 8912896 | tf_op jit(solution)/shard_map/all_gather | solution.py:100
  8.0 189.3 %all-gather.9.cloned.1.call-start = ((), (), s32[]{:S(2)}) async-start(), calls=%async_computation.6 | async-start | bytes 8912896 | tf_op jit(solution)/shard_map/all_gather | solution.py:101
  8.7 263.8 %all-gather.11.cloned.1.call-start = ((), (), s32[]{:S(2)}) async-start(), calls=%async_computation.7 | async-start | bytes 8912896 | tf_op jit(solution)/shard_map/all_gather | solution.py:102
  44.8 152.5 %copy-start.4 = (bf16[256,4096]{1,0:T(8,128)(2,1)S(1)}, bf16[256,4096]{1,0:T(8,128)(2,1)}, u32[]{:S(2)}) copy-start(bf16[256,4096]{1,0:T(8,128)(2,1)} %all-gather.5.cloned.1.call-done) | copy-start | bytes 6291460
  278.3 4.2 collective-permute-start
  283.9 2.3 copy-start
  283.9 2.0 copy-start.2
  287.7 54.9 %all-to-all-start = ((f32[2,16,16,1024]{3,2,0,1:T(8,128)}), f32[2,16,16,1024]{3,2,0,1:T(8,128)S(1)}, u32[]{:S(2)}, u32[]{:S(2)}) async-start(f32[2,16,16,1024]{3,2,0,1:T(8,128)} %copy.34), calls=%async_computation | async-start | bytes 4194304 | tf_op jit(solution)/shard_map/all_to_all | solution.py:23
  379.3 189.0 %all-to-all-start.1 = ((f32[8,16,16,1024]{3,2,0,1:T(8,128)}), f32[8,16,16,1024]{3,2,0,1:T(8,128)}, u32[]{:S(2)}, u32[]{:S(2)}) async-start(f32[8,16,16,1024]{3,2,0,1:T(8,128)} %copy.42), calls=%async_computation.1 | async-start | bytes 16777216 | tf_op jit(solution)/shard_map/all_to_all | solution.py:23
  726.5 30.9 %copy-start.1 = (f32[3,256,1024]{2,1,0:T(8,128)S(1)}, f32[3,256,1024]{2,1,0:T(8,128)}, u32[]{:S(2)}) copy-start(f32[3,256,1024]{2,1,0:T(8,128)} %copy-done) | copy-start | bytes 9437188
  726.5 30.9 %copy-start.3 = (f32[1024]{0:T(1024)S(1)}, f32[1024]{0:T(1024)}, u32[]{:S(2)}) copy-start(f32[1024]{0:T(1024)} %param.13) | copy-start | bytes 12292
Sparse Core Ops, SparseCore 0:
  8.9 35.8 all-gather.4
  47.0 74.8 all-gather.6
  124.1 73.1 all-gather.8
  199.3 73.1 all-gather.10
where the time goes:
time: 772 us; the launch traced here: 766 us
  waiting for transfers between devices  487 us (63%)
  blocking collectives  128 us (17%)
  matrix products  81.6 us (11%)
  local copies, waits for them, and re-layouts  35.7 us (5%)
  between operations  13.9 us (2%)
  starting transfers between devices  13.4 us (2%)
    all_to_all x2, waiting for transfers between devices, regroup(): lax.all_to_all(stacked, ('fsdp', 'ctx'), split_axis=1, concat_axis=1, til...  233 us
    all_to_all x2, blocking collectives, regroup(): lax.all_to_all(stacked, ('fsdp', 'ctx'), split_axis=1, concat_axis=1, til...  128 us
    all_gather x1, waiting for transfers between devices, on_device(): lax.all_gather(w_query, ('fsdp', 'ctx'), axis=0, tiled=True)  77.1 us
    all_gather x1, waiting for transfers between devices, on_device(): lax.all_gather(w_value, ('fsdp', 'ctx'), axis=0, tiled=True)  69.5 us
    all_gather x1, waiting for transfers between devices, on_device(): lax.all_gather(w_key, ('fsdp', 'ctx'), axis=0, tiled=True)  69 us
    all_gather x1, waiting for transfers between devices, on_device(): gathered = lax.all_gather(tokens, 'ch', axis=1, tiled=True)  34.5 us
    another operation x1, local copies, waits for them, and re-layouts, spread_conv(): jnp.stack([real_twist, imag_twist], axis=1)  17.4 us
  transfers between devices with their start and end apart: 7, of which 7 were waited for; matrix products, arithmetic and copies ran while one was open for 2% of the time, Pallas kernels for 0%

commit v1 on v0

v1 whole, which is shorter than its diff:
```python
import functools
import math

import jax
import jax.numpy as jnp
from jax import lax
from jax.experimental import pallas as pl
from jax.experimental.pallas import tpu as pltpu
from jax.sharding import Mesh, PartitionSpec as P

LANES = 128
STEP = 64
WIDE = 512
HALO = 16
ROWS = ("fr", "fc", "cr", "cc")
F32 = jnp.float32
BF16 = jnp.bfloat16


def swap(x, axis, bits):
    size = lax.axis_size(axis)
    return lax.ppermute(x, axis, [(i, i ^ bits) for i in range(size)])


def put(buffer, piece, starts):
    return lax.dynamic_update_slice(buffer, piece, [jnp.int32(s) for s in starts])


def toeplitz_body(h_ref, t_ref):
    channels, chunks, _ = h_ref.shape
    sub = lax.broadcasted_iota(jnp.int32, (STEP, LANES), 0)
    lane = lax.broadcasted_iota(jnp.int32, (STEP, LANES), 1)
    keep = lane >= sub
    for c in range(channels):
        last = jnp.zeros((STEP, LANES), F32)
        for j in range(chunks):
            row = jnp.broadcast_to(h_ref[c, j : j + 1, :].astype(F32), (STEP, LANES))
            now = pltpu.roll(row, 0, 1, stride=1, stride_axis=0)
            block, part = divmod(j, WIDE // LANES)
            t_ref[c, block * STEP : (block + 1) * STEP, part * LANES : (part + 1) * LANES] = jnp.where(
                keep, now, last
            ).astype(BF16)
            last = now


def toeplitz(filters):
    channels, chunks, _ = filters.shape
    depth = chunks * LANES // WIDE * STEP
    group = min(4, channels)
    return pl.pallas_call(
        toeplitz_body,
        grid=(channels // group,),
        in_specs=[pl.BlockSpec((group, chunks, LANES), lambda i: (i, 0, 0))],
        out_specs=pl.BlockSpec((group, depth, WIDE), lambda i: (i, 0, 0)),
        out_shape=jax.ShapeDtypeStruct((channels, depth, WIDE), BF16),
        compiler_params=pltpu.CompilerParams(vmem_limit_bytes=60 << 20),
        cost_estimate=pl.CostEstimate(
            flops=channels * depth * WIDE * 4, bytes_accessed=channels * depth * WIDE * 2, transcendentals=0
        ),
        name="toeplitz",
    )(filters)


def down(x, rows):
    at = lax.broadcasted_iota(jnp.int32, x.shape, 0)
    return jnp.where(at >= rows, pltpu.roll(x, rows, 0), 0.0)


def conv_body(keys, sizes, place, *refs):
    pieces = dict(zip(keys, refs))
    t_ref, bias_ref, o_ref, held, folded = refs[len(keys) :]
    fr_n, fc_n, cr_n, cc_n = sizes
    channels = bias_ref.shape[0]
    rows = folded.shape[0] // channels
    lag = WIDE // STEP
    low = lax.broadcasted_iota(jnp.int32, (channels, LANES), 1) < STEP
    low_rows = lax.broadcasted_iota(jnp.int32, (rows, LANES), 1) < STEP
    bias = bias_ref[...]
    held[0 : lag * channels, :] = jnp.zeros((lag * channels, LANES), F32)

    def spans():
        for (d, a), ref in pieces.items():
            for f in range(fc_n):
                for c in range(cc_n):
                    span = (((place[0] ^ d) * fc_n + f) * cr_n + (place[2] ^ a)) * cc_n + c
                    yield span, ref[f * cc_n + c].astype(F32)

    def lines(row):
        return pl.ds(pl.multiple_of(row * channels, channels), channels)

    for span, gated in spans():
        for k in range(4):
            half = gated[:, (k // 2) * LANES : (k // 2 + 1) * LANES]
            other = pltpu.roll(half, STEP, 1)
            twice = jnp.where(low, half, other) if k % 2 == 0 else jnp.where(low, other, half)
            held[lines(lag + 4 * span + k), :] = twice
    for c in range(channels):
        line = held[pl.ds(c, rows + lag, stride=channels), :]
        pair = jnp.where(low_rows, line[lag:], line[:rows]).astype(BF16)
        parts = [pair]
        for q in range(1, rows // (2 * lag)):
            shift = 2 * lag * q
            parts.append(jnp.concatenate([jnp.zeros((shift, LANES), BF16), pair[: rows - shift]], axis=0))
        left = jnp.concatenate(parts, axis=1)
        wide = jnp.dot(left, t_ref[c], preferred_element_type=F32)
        half_wide = WIDE // 2
        wide = wide[:, :half_wide] + down(wide[:, half_wide:], half_wide // STEP)
        wide = wide[:, :LANES] + down(wide[:, LANES:], 2)
        folded[pl.ds(c, rows, stride=channels), :] = wide + down(pltpu.roll(wide, STEP, 1), 1)
    for span, gated in spans():
        parts = [folded[lines(4 * span + k), :] for k in range(4)]
        for k in range(2):
            conv = jnp.where(low, parts[2 * k], pltpu.roll(parts[2 * k + 1], STEP, 1))
            cut = slice(k * LANES, (k + 1) * LANES)
            o_ref[span, :, cut] = (conv + bias * gated[:, cut]).astype(BF16)


def long_conv(place, pieces, blocks, bias, sizes):
    few, depth = blocks.shape[:2]
    count = math.prod(sizes)
    some = next(iter(pieces.values()))
    span = some.shape[2]
    group = min(16, few)
    rows = count * span // STEP
    return pl.pallas_call(
        functools.partial(conv_body, tuple(pieces), sizes),
        grid=(few // group,),
        in_specs=[
            pl.BlockSpec(memory_space=pltpu.SMEM),
            *[pl.BlockSpec((some.shape[0], group, span), lambda i: (0, i, 0)) for _ in pieces],
            pl.BlockSpec((group, depth, WIDE), lambda i: (i, 0, 0)),
            pl.BlockSpec((group, LANES), lambda i: (i, 0)),
        ],
        out_specs=pl.BlockSpec((count, group, span), lambda i: (0, i, 0)),
        out_shape=jax.ShapeDtypeStruct((count, few, span), BF16),
        scratch_shapes=[
            pltpu.VMEM(((rows + WIDE // STEP) * group, LANES), F32),
            pltpu.VMEM((rows * group, LANES), F32),
        ],
        compiler_params=pltpu.CompilerParams(vmem_limit_bytes=60 << 20),
        cost_estimate=pl.CostEstimate(
            flops=2 * few * rows * depth * WIDE, bytes_accessed=few * depth * WIDE * 2, transcendentals=0
        ),
        name="long_conv",
    )(place, *pieces.values(), blocks, jnp.broadcast_to(bias[:, None], (few, LANES)))


def after(x, *others):
    return lax.optimization_barrier((x, *others))[0]


def short_conv(values, taps):
    return taps[0:1] * values + taps[1:2] * pltpu.roll(values, 1, 0) + taps[2:3] * pltpu.roll(values, 2, 0)


def project_body(token_cuts, halo_cuts, weight_cuts, out_keys, gate, counts, place, *refs):
    token_refs, weight_refs = refs[: counts[0]], refs[counts[0] : counts[0] + counts[1]]
    taps_ref, *refs = refs[counts[0] + counts[1] :]
    o_refs, (tok, tail, full, made, edge, staged, sems) = refs[: len(out_keys)], refs[len(out_keys) :]
    fr, fc, cr, cc, ch = (place[i] for i in range(5))
    blocks, rows, _ = tok.shape
    fc_n, streams = tail.shape[0], full.shape[0]
    cc_n = blocks // fc_n
    depth = weight_refs[0].shape[3]
    cr_n = 1 + max(a for _, a, _ in weight_cuts)
    feats = token_refs[0].shape[1]

    for (d, a, b), (i, j) in weight_cuts.items():
        for e in range(fc_n):
            at = ((((fr ^ d) * fc_n + (fc ^ e)) * cr_n + (cr ^ a)) * cc_n + (cc ^ b)) * depth
            cut = pl.ds(pl.multiple_of(at, depth), depth)
            pltpu.make_async_copy(weight_refs[i].at[j, e], full.at[:, cut, :], sems.at[blocks]).start()
    for (d, b), (i, start, count) in halo_cuts.items():
        cut = pl.ds(pl.multiple_of((ch ^ b) * feats, feats), feats)
        source = token_refs[i].at[pl.ds(start, count), :]
        pltpu.make_async_copy(source, tail.at[fc ^ d, :, cut], sems.at[blocks + 1]).start()
    for (d, a, b, h), (i, start, count) in token_cuts.items():
        block = (fc ^ d) * cc_n + (cc ^ a)
        cut = pl.ds(pl.multiple_of((ch ^ b) * feats, feats), feats)
        source = token_refs[i].at[pl.ds(start, count), :]
        pltpu.make_async_copy(source, tok.at[block, pl.ds(h * count, count), cut], sems.at[block]).start()
    pltpu.make_async_copy(full, full, sems.at[blocks]).wait()
    pltpu.make_async_copy(tail, tail, sems.at[blocks + 1]).wait()
    for s in range(streams):
        both = jnp.dot(tail[...].reshape(fc_n * HALO, -1), full[s], preferred_element_type=F32)
        edge[s] = both.astype(BF16).astype(F32).reshape(edge.shape[1:])

    def one_block(i, carry):
        block = (fc * cc_n + cc) ^ i
        pltpu.make_async_copy(tok.at[block], tok.at[block], sems.at[block]).wait()

        def one_stream(s, carry):
            part = jnp.dot(tok[block], full[s], preferred_element_type=F32)
            made[s, block] = part.astype(BF16).astype(F32)
            return carry

        return lax.fori_loop(0, streams, one_stream, carry)

    lax.fori_loop(0, blocks, one_block, 0)
    for block in range(blocks):
        f, c = divmod(block, cc_n)
        whole = []
        for s in range(streams):
            head = edge[s, f] if c == 0 else made[s, block - 1, rows - HALO :, :]
            whole.append(jnp.concatenate([head, made[s, block]], axis=0))
        if gate:
            one, two = (short_conv(x, taps_ref[s])[HALO:] for s, x in enumerate(whole))
            gated = (one * two).T.astype(BF16)
            few = staged.shape[2]
            for i in range(staged.shape[0]):
                staged[i, block] = gated[i * few : (i + 1) * few]
        else:
            staged[block] = whole[0].astype(BF16)
    ours, inner = (fr, cr) if gate else (fc, cc)
    copies = []
    for n, (d, a) in enumerate(out_keys):
        at = (ours ^ d) * (cr_n if gate else cc_n) + (inner ^ a)
        copies.append(pltpu.make_async_copy(staged.at[at], o_refs[n], sems.at[blocks + 2 + n]))
        copies[-1].start()
    for copy in copies:
        copy.wait()


def project(place, tokens, weights, taps, others, gate):
    arrays, token_cuts, halo_cuts = tokens
    weight_arrays, weight_cuts = weights
    _, fc_n, streams, depth, own = weight_arrays[0].shape
    rows = token_cuts[0, 0, 0, 0][2]
    blocks = fc_n * (1 + max(a for _, a, _, _ in token_cuts))
    features = arrays[0].shape[1] * (1 + max(b for _, b in halo_cuts))
    out_keys = tuple((d, a) for d in range(others[0]) for a in range(others[1]))
    few = own // len(out_keys)
    out = (blocks, few, rows) if gate else (rows + HALO, own)
    anywhere = pl.BlockSpec(memory_space=pl.ANY)
    operands = [*arrays, *weight_arrays]
    counts = (len(arrays), len(weight_arrays))
    made = pl.pallas_call(
        functools.partial(project_body, token_cuts, halo_cuts, weight_cuts, out_keys, gate, counts),
        in_specs=[
            pl.BlockSpec(memory_space=pltpu.SMEM),
            *[anywhere] * len(operands),
            pl.BlockSpec(memory_space=pltpu.VMEM),
        ],
        out_specs=[anywhere] * len(out_keys),
        out_shape=[jax.ShapeDtypeStruct(out, BF16)] * len(out_keys),
        scratch_shapes=[
            pltpu.VMEM((blocks, rows, features), BF16),
            pltpu.VMEM((fc_n, HALO, features), BF16),
            pltpu.VMEM((streams, features, own), BF16),
            pltpu.VMEM((streams, blocks, rows, own), F32),
            pltpu.VMEM((streams, fc_n, HALO, own), F32),
            pltpu.VMEM((len(out_keys), *out), BF16),
            pltpu.SemaphoreType.DMA((blocks + 2 + len(out_keys),)),
        ],
        compiler_params=pltpu.CompilerParams(vmem_limit_bytes=60 << 20),
        cost_estimate=pl.CostEstimate(
            flops=2 * blocks * rows * features * own * streams,
            bytes_accessed=2 * features * (blocks * rows + own * streams),
            transcendentals=0,
        ),
        name="project",
    )(place, *operands, taps)
    return dict(zip(out_keys, made))


def exchange(pieces, axes):
    second = lax.axis_size(axes[1])
    return {(d, a): x if (d, a) == (0, 0) else swap(x, axes, d * second + a) for (d, a), x in pieces.items()}


def combine_body(keys, sizes, place, *refs):
    fr_n, fc_n, cr_n, cc_n = sizes
    mixed_ref, taps_ref, o_ref, query, turned = refs[len(keys) :]
    own, few = turned.shape[0], mixed_ref.shape[1]
    for (d, a), ref in zip(keys, refs):
        query[(place[1] ^ d) * cc_n + (place[3] ^ a)] = ref[...].astype(F32)
    for f in range(fc_n):
        for c in range(cc_n):
            j = f * cc_n + c
            for x in range(fr_n):
                for z in range(cr_n):
                    at = (x * cr_n + z) * few
                    turned[at : at + few, :] = mixed_ref[((x * fc_n + f) * cr_n + z) * cc_n + c].astype(F32)
            cut = slice(j * own, (j + 1) * own)
            filtered = short_conv(query[j], taps_ref[:, cut])[HALO:]
            o_ref[:, cut] = (filtered * turned[...].T).astype(BF16)


def combine(place, query, mixed, taps, sizes):
    vmem = pl.BlockSpec(memory_space=pltpu.VMEM)
    rows, own = next(iter(query.values())).shape
    span = mixed.shape[2]
    groups = sizes[1] * sizes[3]
    return pl.pallas_call(
        functools.partial(combine_body, tuple(query), sizes),
        in_specs=[pl.BlockSpec(memory_space=pltpu.SMEM)] + [vmem] * (len(query) + 2),
        out_specs=vmem,
        out_shape=jax.ShapeDtypeStruct((span, groups * own), BF16),
        scratch_shapes=[pltpu.VMEM((groups, rows, own), F32), pltpu.VMEM((own, span), F32)],
        compiler_params=pltpu.CompilerParams(vmem_limit_bytes=60 << 20),
        name="combine",
    )(place, *query.values(), mixed, taps)


def tied(arrays, ties):
    return list(lax.optimization_barrier((*arrays, *ties))[: len(arrays)])


def weight_halves(streams, cut):
    fc_n, cc_n = lax.axis_size("fc"), lax.axis_size("cc")
    fc, cc = lax.axis_index("fc"), lax.axis_index("cc")
    wide = streams[0].shape[1] // fc_n
    own = wide // cc_n
    parts = []
    for e in range(fc_n):
        part = jnp.stack([lax.dynamic_slice_in_dim(w, (fc ^ e) * wide, wide, 1) for w in streams])
        parts.append(part if e == 0 else swap(part, "fc", e))

    def half(b, some):
        return jnp.stack([lax.dynamic_slice_in_dim(p[some], (cc ^ b) * own, own, 2) for p in parts])[None]

    return [[half(b, some) for b in range(cc_n)] for some in (slice(None, cut), slice(cut, None))]


def on_device(tokens, w_query, w_key, w_value, short_taps, long_filter, filter_bias):
    fr_n, fc_n, cr_n, cc_n = (lax.axis_size(a) for a in ROWS)
    fr, fc, cr, cc = (lax.axis_index(a) for a in ROWS)
    ch_n, ch = lax.axis_size("ch"), lax.axis_index("ch")
    rows = tokens.shape[0]
    part = rows // 2
    channels = w_query.shape[1]
    count = fr_n * fc_n * cr_n * cc_n
    total = count * rows
    own = channels // (cc_n * fc_n)
    few = own // (fr_n * cr_n)
    sizes = (fr_n, fc_n, cr_n, cc_n)
    place = jnp.stack([fr, fc, cr, cc, ch]).astype(jnp.int32)
    ctx = ("cr", "cc")
    first, second = [2, 1], list(range(3, cr_n * cc_n))

    def along_y(x):
        return [swap(x, "ch", b) for b in range(1, ch_n)]

    def along_x(x):
        return [swap(x, "fr", d) for d in range(1, fr_n)]

    kv, q = weight_halves([w_key, w_value, w_query], 2)
    halo = lax.ppermute(tokens[-HALO:], ROWS, [(i, i + 1) for i in range(count - 1)])
    cc_low = swap(tokens[:part], "cc", 1)
    y_own = along_y(tokens)
    kv_first = [swap(kv[k % cc_n], ctx, k) for k in first]
    kv_x0 = along_x(kv[0])
    lags = after(long_filter, *kv_x0).astype(BF16).T.reshape(fc_n, cc_n, fr_n, cr_n, few, rows)
    lags = lags.transpose(2, 0, 3, 1, 4, 5).reshape(count, few, rows)
    lags = lax.all_to_all(lags, ROWS, split_axis=0, concat_axis=0, tiled=True)
    ties = [halo, cc_low, *y_own, *kv_first, *kv_x0, lags]

    high, low, mine, kv_low, kv_high, near, lags = tied(
        [
            jnp.concatenate([tokens[part:], halo]),
            cc_low,
            jnp.concatenate([tokens, *y_own]),
            kv[0],
            kv[1],
            jnp.concatenate(kv_first),
            lags,
        ],
        ties,
    )
    kv_second = [swap((kv_low, kv_high)[k % cc_n], ctx, k) for k in second]
    kv_x1 = along_x(near)
    cc_high = swap(high, "cc", 1)
    y_low = along_y(low)
    core_own = swap(mine, "fc", 1)
    blocks = toeplitz(lags.transpose(1, 0, 2).reshape(few, total // LANES, LANES))
    ties = [*kv_second, *kv_x1, cc_high, *y_low, core_own, blocks]

    edge = jnp.where(cc == 0, halo, cc_high[part:])
    high, core_low, far, *q = tied(
        [
            jnp.concatenate([cc_high[:part], edge]),
            jnp.concatenate([cc_low, *y_low, cc_high[:part], edge]),
            jnp.concatenate(kv_second),
            *q,
        ],
        ties,
    )
    kv_x2 = along_x(far)
    y_high = along_y(high)
    core_low = swap(core_low, "fc", 1)
    q_first = [swap(q[k % cc_n], ctx, k) for k in first]
    core_high = swap(tied([jnp.concatenate(y_high)], [*kv_x2, *q_first, core_low])[0], "fc", 1)
    ties = [*kv_x2, *y_high, core_low, *q_first, core_high]

    arrays = [tokens, *y_own, core_own, cc_low, *y_low, high, *y_high, core_low, core_high]
    token_cuts, halo_cuts = {}, {}
    at = {id(x): i for i, x in enumerate(arrays)}
    for b in range(ch_n):
        source = tokens if b == 0 else y_own[b - 1]
        token_cuts[0, 0, b, 0] = (at[id(source)], 0, rows)
        token_cuts[1, 0, b, 0] = (at[id(core_own)], b * rows, rows)
        source = cc_low if b == 0 else y_low[b - 1]
        token_cuts[0, 1, b, 0] = (at[id(source)], 0, part)
        token_cuts[1, 1, b, 0] = (at[id(core_low)], b * part, part)
        source = high if b == 0 else y_high[b - 1]
        token_cuts[0, 1, b, 1] = (at[id(source)], 0, part)
        halo_cuts[0, b] = (at[id(source)], part, HALO)
        source, start = (core_low, ch_n * part) if b == 0 else (core_high, (b - 1) * (part + HALO))
        token_cuts[1, 1, b, 1] = (at[id(source)], start, part)
        halo_cuts[1, b] = (at[id(source)], start + part, HALO)
    held = (arrays, token_cuts, halo_cuts)

    def weights_of(own_piece, firsts, seconds, xs):
        sets = [([0], [own_piece]), (first, firsts), (second, seconds)]
        operands, cuts = [], {}
        for (partners, pieces), others in zip(sets, xs):
            for i, (k, piece) in enumerate(zip(partners, pieces)):
                cuts[(0, *divmod(k, cc_n))] = (len(operands), 0)
                operands.append(piece)
            for d, other in enumerate(others, 1):
                for i, k in enumerate(partners):
                    cuts[(d, *divmod(k, cc_n))] = (len(operands), i)
                operands.append(other)
        return operands, cuts

    group = (fc * cc_n + cc) * own
    taps = lax.dynamic_slice_in_dim(short_taps, group, own, 2)
    weights = weights_of(kv[0], kv_first, kv_second, (kv_x0, kv_x1, kv_x2))
    gated = project(place, held, weights, taps[1:], (fr_n, cr_n), True)
    near, *q = tied([jnp.concatenate(q_first), *q], ties)
    q_second = [swap(q[k % cc_n], ctx, k) for k in second]
    q_x0 = along_x(near)
    ties = [*q_second, *q_x0]
    keys = list(gated)
    *pieces, far = tied([*gated.values(), jnp.concatenate([q[0], *q_second])], ties)
    gated = exchange(dict(zip(keys, pieces)), ("fr", "cr"))
    q_x1 = along_x(after(far, *gated.values()))

    bias = lax.dynamic_slice_in_dim(filter_bias, group + (fr * cr_n + cr) * few, few, 0)
    mixed = long_conv(place, gated, blocks, bias, sizes)
    place, mixed = tied([place, mixed], q_x1)
    mixed = lax.all_to_all(mixed, ROWS, split_axis=0, concat_axis=0, tiled=True)

    pieces = [*q_first, q[0], *q_second]
    operands, cuts = [*pieces, *q_x0, *q_x1], {}
    for i, k in enumerate([*first, 0, *second]):
        cuts[(0, *divmod(k, cc_n))] = (i, 0)
        for d in range(1, fr_n):
            late = i >= len(first)
            at = len(pieces) + d - 1 + (fr_n - 1 if late else 0)
            cuts[(d, *divmod(k, cc_n))] = (at, i - len(first) if late else i)
    query = project(place, held, (operands, cuts), taps[:1], (fc_n, cc_n), False)
    query = exchange(query, ("fc", "cc"))
    return combine(place, query, mixed, short_taps[0], sizes)


def solution(mesh):
    f, x, h = (mesh.shape[a] for a in ("fsdp", "ctx", "ch"))
    fine = Mesh(mesh.devices.reshape(f // 2, 2, x // 2, 2, h), ROWS + ("ch",))
    spec = P(ROWS, "ch")
    return jax.shard_map(
        on_device,
        mesh=fine,
        in_specs=(spec, spec, spec, spec, P(None, None, "ch"), spec, P("ch")),
        out_specs=spec,
        check_vma=False,
    )
```

time: 772 us -> 184 us (0.24)
  waiting for transfers between devices: 487 us -> 63.2 us
  blocking collectives: 128 us -> 0 us
  matrix products: 81.6 us -> 0 us
  Pallas kernels: 0 us -> 54.3 us
  starting transfers between devices: 13.4 us -> 39.8 us
  local copies, waits for them, and re-layouts: 35.7 us -> 15.6 us
  between operations: 13.9 us -> 0.39 us
    all_gather x4 -> x0, waiting for transfers between devices: 250 us -> none  [the longest x1 77.1 us: on_device(): lax.all_gather(w_query, ('fsdp', 'ctx'), axis=0, tiled=True)]
    all_to_all x2, waiting for transfers between devices: 233 us -> 0.01 us  [the longest x1 0.01 us: on_device(): lags = lax.all_to_all(lags, ROWS, split_axis=0, concat_axis=0, tiled=True)]
    all_to_all x2 -> x0, blocking collectives: 128 us -> none  [regroup(): lax.all_to_all(stacked, ('fsdp', 'ctx'), split_axis=1, concat_axis=1, til...]
    dot_general x15 -> x0, matrix products: 81.6 us -> none  [the longest x1 8.4 us: spread_conv(): jnp.einsum('kn,bsnc->bskc', sin_row, spread[:, 0], precision=HIGHEST)]
    ppermute x1 -> x27, waiting for transfers between devices: 1.35 us -> 63.2 us  [the longest x26 63.2 us: swap(): return lax.ppermute(x, axis, [(i, i ^ bits) for i in range(size)])]
    pallas_call x0 -> x5, Pallas kernels: none -> 54.3 us  [the longest x2 19.9 us: project(): pl.pallas_call(functools.partial(project_body, token_cuts, halo_cuts, wei...]
    ppermute x1 -> x27, starting transfers between devices: 2.8 us -> 29.7 us  [the longest x26 26.2 us: swap(): return lax.ppermute(x, axis, [(i, i ^ bits) for i in range(size)])]
    another operation x2 -> x6, local copies, waits for them, and re-layouts: 18.9 us -> 4.2 us  [the longest x2 2.23 us: weight_halves(): jnp.stack([lax.dynamic_slice_in_dim(w, (fc ^ e) * wide, wide, 1) for w in...]
  transfers between devices with their start and end apart: 7 -> 29, of which waited for: 7 -> 14; matrix products, arithmetic and copies ran while one was open for 2% -> 11% of each run, Pallas kernels for 0% -> 28%
where the time goes in v1:
time: 184 us; the launch traced here: 183 us
  waiting for transfers between devices  63.2 us (34%)
  Pallas kernels  54.3 us (30%)
  starting transfers between devices  39.8 us (22%)
  local copies, waits for them, and re-layouts  15.6 us (8%)
  other arithmetic  9.87 us (5%)
    ppermute x26, waiting for transfers between devices, swap(): return lax.ppermute(x, axis, [(i, i ^ bits) for i in range(size)])  63.2 us
    ppermute x26, starting transfers between devices, swap(): return lax.ppermute(x, axis, [(i, i ^ bits) for i in range(size)])  26.2 us
    pallas_call x2, Pallas kernels, project(): pl.pallas_call(functools.partial(project_body, token_cuts, halo_cuts, wei...  19.9 us
    pallas_call x1, Pallas kernels, toeplitz(): pl.pallas_call(toeplitz_body, grid=(channels // group,), in_specs=[pl.Blo...  17.4 us
    pallas_call x1, Pallas kernels, long_conv(): pl.pallas_call(functools.partial(conv_body, tuple(pieces), sizes), grid=(...  14.4 us
    all_to_all x1, starting transfers between devices, on_device(): lags = lax.all_to_all(lags, ROWS, split_axis=0, concat_axis=0, tiled=True)  6.16 us
    all_to_all x1, starting transfers between devices, on_device(): mixed = lax.all_to_all(mixed, ROWS, split_axis=0, concat_axis=0, tiled=True)  3.95 us
  transfers between devices with their start and end apart: 29, of which 14 were waited for; matrix products, arithmetic and copies ran while one was open for 11% of the time, Pallas kernels for 28%

profile of v1, /device:TPU:0, one launch (start us, length us, event | category | flops | bytes accessed | tf_op | source)
XLA Modules:
  0.0 183.2 jit_solution(10452281053728519185)
XLA Ops:
  5.9 2.9 %collective-permute-start.6 = (bf16[1,2,2,256,256]{4,3,2,1,0:T(8,128)(2,1)}, bf16[1,2,2,256,256]{4,3,2,1,0:T(8,128)(2,1)}, u32[]{:S(2)}, u32[]{:S(2)}) collective-permute-start(bf16[1,2,2,256,256]{4,3,2,1,0:T(8,128)(2,1)} %maximum_bitcast_fusion.refs_9_), channel_id=1, source_target_pairs={{0,16},{16,0},{1,17},{17,1},{2,18},{18,2},{3,19},{19,3},{4,20},{20... | collective-permute-start | bytes 1572872 | tf_op jit(solution)/shard_map/ppermute | solution.py:22
  10.3 3.5 %collective-permute-start.1 = (bf16[16,2048]{1,0:T(8,128)(2,1)S(1)}, bf16[16,2048]{1,0:T(8,128)(2,1)S(1)}, u32[]{:S(2)}, u32[]{:S(2)}) collective-permute-start(bf16[16,2048]{1,0:T(8,128)(2,1)S(1)} %slice.37), channel_id=1, source_target_pairs={{0,2},{2,4},{4,6},{6,8},{8,10},{10,12},{12,14},{14,16},{16,18},{18... | collective-permute-start | bytes 196616 | tf_op jit(solution)/shard_map/ppermute | solution.py:348
  13.8 2.7 %collective-permute-start.4 = (bf16[1,2,2,256,256]{4,3,2,1,0:T(8,128)(2,1)}, bf16[1,2,2,256,256]{4,3,2,1,0:T(8,128)(2,1)}, u32[]{:S(2)}, u32[]{:S(2)}) collective-permute-start(bf16[1,2,2,256,256]{4,3,2,1,0:T(8,128)(2,1)} %maximum_bitcast_fusion.refs_9_), channel_id=1, source_target_pairs={{0,4},{2,6},{4,0},{6,2},{1,5},{3,7},{5,1},{7,3},{8,12},{10,14},{12... | collective-permute-start | bytes 1572872 | tf_op jit(solution)/shard_map/ppermute | solution.py:22
  17.3 4.0 %collective-permute-done.6.refs_10_ = bf16[1,2,2,256,256]{4,3,2,1,0:T(8,128)(2,1)} collective-permute-done((bf16[1,2,2,256,256]{4,3,2,1,0:T(8,128)(2,1)}, bf16[1,2,2,256,256]{4,3,2,1,0:T(8,128)(2,1)}, u32[]{:S(2)}, u32[]{:S(2)}) %collective-permute-start.6) | collective-permute-done | bytes 524320 | tf_op jit(solution)/shard_map/ppermute | solution.py:22
  23.6 6.2 %all-to-all-start = ((bf16[16,64,256]{2,1,0:T(8,128)(2,1)}), bf16[16,64,256]{2,1,0:T(8,128)(2,1)S(1)}, u32[]{:S(2)}, u32[]{:S(2)}) async-start(bf16[16,64,256]{2,1,0:T(8,128)(2,1)} %bitcast.19), calls=%async_computation | async-start | bytes 1048576 | tf_op jit(solution)/shard_map/all_to_all | solution.py:355
  29.8 2.0 %collective-permute-start.2 = (bf16[128,2048]{1,0:T(8,128)(2,1)S(1)}, bf16[128,2048]{1,0:T(8,128)(2,1)S(1)}, u32[]{:S(2)}, u32[]{:S(2)}) collective-permute-start(bf16[128,2048]{1,0:T(8,128)(2,1)S(1)} %get-tuple-element.69), channel_id=1, source_target_pairs={{0,2},{2,0},{1,3},{3,1},{4,6},{6,4},{5,7},{7,5},{8,10},{10,8},{9,1... | collective-permute-start | bytes 1572872 | tf_op jit(solution)/shard_map/ppermute | solution.py:22
  35.2 7.1 %collective-permute-done.5.refs_12_ = bf16[1,2,2,256,256]{4,3,2,1,0:T(8,128)(2,1)} collective-permute-done((bf16[1,2,2,256,256]{4,3,2,1,0:T(8,128)(2,1)}, bf16[1,2,2,256,256]{4,3,2,1,0:T(8,128)(2,1)}, u32[]{:S(2)}, u32[]{:S(2)}) %collective-permute-start.5) | collective-permute-done | bytes 524320 | tf_op jit(solution)/shard_map/ppermute | solution.py:22
  42.3 2.3 %pad_maximum_fusion.2 = bf16[2,2,2,256,256]{4,3,2,1,0:T(8,128)(2,1)} fusion(bf16[1,2,2,256,256]{4,3,2,1,0:T(8,128)(2,1)} %collective-permute-done.5.refs_12_, bf16[1,2,2,256,256]{4,3,2,1,0:T(8,128)(2,1)} %collective-permute-done.4.refs_11_), kind=kLoop, calls=%fused_computation.2 | loop fusion | flops 524288 | bytes 2097152 | tf_op jit(solution)/shard_map/concatenate | solution.py:365
  44.6 16.4 %collective-permute-done.2.refs_3_ = bf16[128,2048]{1,0:T(8,128)(2,1)S(1)} collective-permute-done((bf16[128,2048]{1,0:T(8,128)(2,1)S(1)}, bf16[128,2048]{1,0:T(8,128)(2,1)S(1)}, u32[]{:S(2)}, u32[]{:S(2)}) %collective-permute-start.2) | collective-permute-done | bytes 524320 | tf_op jit(solution)/shard_map/ppermute | solution.py:22
  66.5 2.0 %reshape.16.h_ref = bf16[64,32,128]{2,1,0:T(8,128)(2,1)} reshape(bf16[64,16,256]{2,1,0:T(8,128)(2,1)} %copy.12) | data formatting | bytes 1048576 | tf_op jit(solution)/shard_map/reshape | solution.py:375
  68.5 17.4 %toeplitz.1.refs_4_ = bf16[64,512,512]{2,1,0:T(8,128)(2,1)} custom-call(bf16[64,32,128]{2,1,0:T(8,128)(2,1)} %reshape.16.h_ref), custom_call_target="tpu_custom_call" | custom-call | flops 67108864 | bytes 33554432 | tf_op jit(solution)/shard_map/toeplitz/pallas_call | solution.py:50
  85.9 2.4 %collective-permute-done.9 = bf16[144,2048]{1,0:T(8,128)(2,1)} collective-permute-done((bf16[144,2048]{1,0:T(8,128)(2,1)}, bf16[144,2048]{1,0:T(8,128)(2,1)}, u32[]{:S(2)}, u32[]{:S(2)}) %collective-permute-start.9) | collective-permute-done | bytes 589856 | tf_op jit(solution)/shard_map/ppermute | solution.py:22
  95.9 11.6 %collective-permute-done.15.refs_9_ = bf16[1,2,1,256,256]{4,3,2,1,0:T(8,128)(2,1)S(1)} collective-permute-done((bf16[1,2,1,256,256]{4,3,2,1,0:T(8,128)(2,1)S(1)}, bf16[1,2,1,256,256]{4,3,2,1,0:T(8,128)(2,1)S(1)}, u32[]{:S(2)}, u32[]{:S(2)}) %collective-permute-start.15) | collective-permute-done | bytes 262176 | tf_op jit(solution)/shard_map/ppermute | solution.py:22
  110.7 2.4 %collective-permute-start.18 = (bf16[1,2,1,256,256]{4,3,2,1,0:T(8,128)(2,1)}, bf16[1,2,1,256,256]{4,3,2,1,0:T(8,128)(2,1)S(1)}, u32[]{:S(2)}, u32[]{:S(2)}) collective-permute-start(bf16[1,2,1,256,256]{4,3,2,1,0:T(8,128)(2,1)} %maximum_bitcast_fusion.3), channel_id=1, source_target_pairs={{0,6},{2,4},{4,2},{6,0},{1,7},{3,5},{5,3},{7,1},{8,14},{10,12},{12... | collective-permute-start | bytes 786440 | tf_op jit(solution)/shard_map/ppermute | solution.py:22
  113.4 12.0 %project.2 = (bf16[4,64,256]{2,1,0:T(8,128)(2,1)}, bf16[4,64,256]{2,1,0:T(8,128)(2,1)}, bf16[4,64,256]{2,1,0:T(8,128)(2,1)}, bf16[4,64,256]{2,1,0:T(8,128)(2,1)}) custom-call(s32[5]{0:T(128)} %stack.81.place, bf16[256,2048]{1,0:T(8,128)(2,1)} %refs_0_.3, bf16[256,2048]{1,0:T(8,128)(2,1)} %copy-done.1, bf16[512,2048]{1,0:T(8,128)(2,1)} %copy-done.4, ...), custom_call_target="tpu_custom_call" | custom-call | flops 4294967296 | bytes 12582912 | tf_op jit(solution)/shard_map/project/pallas_call | solution.py:237
  127.4 3.9 %collective-permute-start.22 = (bf16[4,64,256]{2,1,0:T(8,128)(2,1)}, bf16[4,64,256]{2,1,0:T(8,128)(2,1)S(1)}, u32[]{:S(2)}, u32[]{:S(2)}) collective-permute-start(bf16[4,64,256]{2,1,0:T(8,128)(2,1)} %get-tuple-element.60), channel_id=1, source_target_pairs={{0,20},{4,16},{16,4},{20,0},{1,21},{5,17},{17,5},{21,1},{2,22},{6,... | collective-permute-start | bytes 393224 | tf_op jit(solution)/shard_map/ppermute | solution.py:22
  131.3 6.5 %collective-permute-done.20.refs_1_ = bf16[4,64,256]{2,1,0:T(8,128)(2,1)S(1)} collective-permute-done((bf16[4,64,256]{2,1,0:T(8,128)(2,1)}, bf16[4,64,256]{2,1,0:T(8,128)(2,1)S(1)}, u32[]{:S(2)}, u32[]{:S(2)}) %collective-permute-start.20) | collective-permute-done | bytes 131104 | tf_op jit(solution)/shard_map/ppermute | solution.py:22
  137.8 2.5 %collective-permute-done.22.refs_3_ = bf16[4,64,256]{2,1,0:T(8,128)(2,1)S(1)} collective-permute-done((bf16[4,64,256]{2,1,0:T(8,128)(2,1)}, bf16[4,64,256]{2,1,0:T(8,128)(2,1)S(1)}, u32[]{:S(2)}, u32[]{:S(2)}) %collective-permute-start.22) | collective-permute-done | bytes 131104 | tf_op jit(solution)/shard_map/ppermute | solution.py:22
  142.8 14.4 %long_conv.1 = bf16[16,64,256]{2,1,0:T(8,128)(2,1)} custom-call(s32[5]{0:T(128)} %stack.81.place, bf16[4,64,256]{2,1,0:T(8,128)(2,1)} %get-tuple-element.57.refs_0_, bf16[4,64,256]{2,1,0:T(8,128)(2,1)} %copy-done.16, bf16[4,64,256]{2,1,0:T(8,128)(2,1)} %copy-done.17, bf16[4,64,256]{2,1,0:T(8,128)(2,1)} %copy-done.18, bf16[64,512,512]{2,1,0:T(8,128)(2,1)} %toeplitz.1.refs_4_, ...), custom_call_target="tpu_custom_call" | custom-call | flops 2147483648 | bytes 33554432 | tf_op jit(solution)/shard_map/long_conv/pallas_call | solution.py:125
  157.2 3.9 %all-to-all-start.1 = ((bf16[16,64,256]{2,1,0:T(8,128)(2,1)}), bf16[16,64,256]{2,1,0:T(8,128)(2,1)S(1)}, u32[]{:S(2)}, u32[]{:S(2)}) async-start(bf16[16,64,256]{2,1,0:T(8,128)(2,1)} %long_conv.1), calls=%async_computation.1 | async-start | bytes 1048576 | tf_op jit(solution)/shard_map/all_to_all | solution.py:442
  161.8 7.9 %project.3 = (bf16[272,256]{1,0:T(8,128)(2,1)}, bf16[272,256]{1,0:T(8,128)(2,1)}, bf16[272,256]{1,0:T(8,128)(2,1)}, bf16[272,256]{1,0:T(8,128)(2,1)}) custom-call(s32[5]{0:T(128)} %stack.81.place, bf16[256,2048]{1,0:T(8,128)(2,1)} %refs_0_.3, bf16[256,2048]{1,0:T(8,128)(2,1)} %copy-done.1, bf16[512,2048]{1,0:T(8,128)(2,1)} %copy-done.4, ...), custom_call_target="tpu_custom_call" | custom-call | flops 2147483648 | bytes 10485760 | tf_op jit(solution)/shard_map/project/pallas_call | solution.py:237
  172.5 4.8 %collective-permute-done.24.refs_1_ = bf16[272,256]{1,0:T(8,128)(2,1)S(1)} collective-permute-done((bf16[272,256]{1,0:T(8,128)(2,1)}, bf16[272,256]{1,0:T(8,128)(2,1)S(1)}, u32[]{:S(2)}, u32[]{:S(2)}) %collective-permute-start.24) | collective-permute-done | bytes 139296 | tf_op jit(solution)/shard_map/ppermute | solution.py:22
  177.3 2.4 %collective-permute-done.26.refs_3_ = bf16[272,256]{1,0:T(8,128)(2,1)S(1)} collective-permute-done((bf16[272,256]{1,0:T(8,128)(2,1)}, bf16[272,256]{1,0:T(8,128)(2,1)S(1)}, u32[]{:S(2)}, u32[]{:S(2)}) %collective-permute-start.26) | collective-permute-done | bytes 139296 | tf_op jit(solution)/shard_map/ppermute | solution.py:22
  180.5 2.6 %combine.1 = bf16[256,1024]{1,0:T(8,128)(2,1)} custom-call(s32[5]{0:T(128)} %stack.81.place, bf16[272,256]{1,0:T(8,128)(2,1)} %get-tuple-element.64.refs_0_, bf16[272,256]{1,0:T(8,128)(2,1)} %copy-done.13, bf16[272,256]{1,0:T(8,128)(2,1)} %copy-done.14, bf16[272,256]{1,0:T(8,128)(2,1)} %copy-done.15, bf16[16,64,256]{2,1,0:T(8,128)(2,1)} %copy-done.6, ...), custom_call_target="tpu_custom_call" | custom-call | tf_op jit(solution)/shard_map/combine/pallas_call | solution.py:294
  (116 shorter events, 39.1 us)
Async XLA Ops:
  5.9 15.4 %collective-permute-start.6 = (bf16[1,2,2,256,256]{4,3,2,1,0:T(8,128)(2,1)}, bf16[1,2,2,256,256]{4,3,2,1,0:T(8,128)(2,1)}, u32[]{:S(2)}, u32[]{:S(2)}) collective-permute-start(bf16[1,2,2,256,256]{4,3,2,1,0:T(8,128)(2,1)} %maximum_bitcast_fusion.refs_9_), channel_id=1, source_target_pairs={{0,16},{16,0},{1,17},{17,1},{2,18},{18,2},{3,19},{19,3},{4,20},{20... | collective-permute-start | bytes 1572872 | tf_op jit(solution)/shard_map/ppermute | solution.py:22
  8.8 24.9 %collective-permute-start = (bf16[256,2048]{1,0:T(8,128)(2,1)S(1)}, bf16[256,2048]{1,0:T(8,128)(2,1)S(1)}, u32[]{:S(2)}, u32[]{:S(2)}) collective-permute-start(bf16[256,2048]{1,0:T(8,128)(2,1)S(1)} %copy-done), channel_id=1, source_target_pairs={{0,1},{1,0},{2,3},{3,2},{4,5},{5,4},{6,7},{7,6},{8,9},{9,8},{10,11... | collective-permute-start | bytes 3145736 | tf_op jit(solution)/shard_map/ppermute | solution.py:22
  10.3 21.5 %collective-permute-start.1 = (bf16[16,2048]{1,0:T(8,128)(2,1)S(1)}, bf16[16,2048]{1,0:T(8,128)(2,1)S(1)}, u32[]{:S(2)}, u32[]{:S(2)}) collective-permute-start(bf16[16,2048]{1,0:T(8,128)(2,1)S(1)} %slice.37), channel_id=1, source_target_pairs={{0,2},{2,4},{4,6},{6,8},{8,10},{10,12},{12,14},{14,16},{16,18},{18... | collective-permute-start | bytes 196616 | tf_op jit(solution)/shard_map/ppermute | solution.py:348
  13.8 28.6 %collective-permute-start.4 = (bf16[1,2,2,256,256]{4,3,2,1,0:T(8,128)(2,1)}, bf16[1,2,2,256,256]{4,3,2,1,0:T(8,128)(2,1)}, u32[]{:S(2)}, u32[]{:S(2)}) collective-permute-start(bf16[1,2,2,256,256]{4,3,2,1,0:T(8,128)(2,1)} %maximum_bitcast_fusion.refs_9_), channel_id=1, source_target_pairs={{0,4},{2,6},{4,0},{6,2},{1,5},{3,7},{5,1},{7,3},{8,12},{10,14},{12... | collective-permute-start | bytes 1572872 | tf_op jit(solution)/shard_map/ppermute | solution.py:22
  17.3 25.1 %collective-permute-start.5 = (bf16[1,2,2,256,256]{4,3,2,1,0:T(8,128)(2,1)}, bf16[1,2,2,256,256]{4,3,2,1,0:T(8,128)(2,1)}, u32[]{:S(2)}, u32[]{:S(2)}) collective-permute-start(bf16[1,2,2,256,256]{4,3,2,1,0:T(8,128)(2,1)} %maximum_bitcast_fusion.1), channel_id=1, source_target_pairs={{0,2},{2,0},{4,6},{6,4},{1,3},{3,1},{5,7},{7,5},{8,10},{10,8},{12,... | collective-permute-start | bytes 1572872 | tf_op jit(solution)/shard_map/ppermute | solution.py:22
  23.6 37.5 %all-to-all-start = ((bf16[16,64,256]{2,1,0:T(8,128)(2,1)}), bf16[16,64,256]{2,1,0:T(8,128)(2,1)S(1)}, u32[]{:S(2)}, u32[]{:S(2)}) async-start(bf16[16,64,256]{2,1,0:T(8,128)(2,1)} %bitcast.19), calls=%async_computation | async-start | bytes 1048576 | tf_op jit(solution)/shard_map/all_to_all | solution.py:355
  29.8 31.2 %collective-permute-start.2 = (bf16[128,2048]{1,0:T(8,128)(2,1)S(1)}, bf16[128,2048]{1,0:T(8,128)(2,1)S(1)}, u32[]{:S(2)}, u32[]{:S(2)}) collective-permute-start(bf16[128,2048]{1,0:T(8,128)(2,1)S(1)} %get-tuple-element.69), channel_id=1, source_target_pairs={{0,2},{2,0},{1,3},{3,1},{4,6},{6,4},{5,7},{7,5},{8,10},{10,8},{9,1... | collective-permute-start | bytes 1572872 | tf_op jit(solution)/shard_map/ppermute | solution.py:22
  61.0 30.8 %collective-permute-start.7 = (bf16[512,2048]{1,0:T(8,128)(2,1)}, bf16[512,2048]{1,0:T(8,128)(2,1)S(1)}, u32[]{:S(2)}, u32[]{:S(2)}) collective-permute-start(bf16[512,2048]{1,0:T(8,128)(2,1)} %pad_maximum_fusion), channel_id=1, source_target_pairs={{0,8},{8,0},{1,9},{9,1},{2,10},{10,2},{3,11},{11,3},{4,12},{12,4},... | collective-permute-start | bytes 6291464 | tf_op jit(solution)/shard_map/ppermute | solution.py:22
  61.0 27.3 %collective-permute-start.9 = (bf16[144,2048]{1,0:T(8,128)(2,1)}, bf16[144,2048]{1,0:T(8,128)(2,1)}, u32[]{:S(2)}, u32[]{:S(2)}) collective-permute-start(bf16[144,2048]{1,0:T(8,128)(2,1)} %pad_maximum_fusion.4), channel_id=1, source_target_pairs={{0,2},{2,0},{1,3},{3,1},{4,6},{6,4},{5,7},{7,5},{8,10},{10,8},{9,1... | collective-permute-start | bytes 1769480 | tf_op jit(solution)/shard_map/ppermute | solution.py:22
  62.5 29.3 %collective-permute-start.11 = (bf16[2,2,2,256,256]{4,3,2,1,0:T(8,128)(2,1)}, bf16[2,2,2,256,256]{4,3,2,1,0:T(8,128)(2,1)}, u32[]{:S(2)}, u32[]{:S(2)}) collective-permute-start(bf16[2,2,2,256,256]{4,3,2,1,0:T(8,128)(2,1)} %pad_maximum_fusion.2), channel_id=1, source_target_pairs={{0,16},{16,0},{1,17},{17,1},{2,18},{18,2},{3,19},{19,3},{4,20},{20... | collective-permute-start | bytes 3145736 | tf_op jit(solution)/shard_map/ppermute | solution.py:22
  63.4 26.9 %collective-permute-start.8 = (bf16[128,2048]{1,0:T(8,128)(2,1)S(1)}, bf16[128,2048]{1,0:T(8,128)(2,1)}, u32[]{:S(2)}, u32[]{:S(2)}) collective-permute-start(bf16[128,2048]{1,0:T(8,128)(2,1)S(1)} %collective-permute-done.2.refs_3_), channel_id=1, source_target_pairs={{0,1},{1,0},{2,3},{3,2},{4,5},{5,4},{6,7},{7,6},{8,9},{9,8},{10,11... | collective-permute-start | bytes 1572872 | tf_op jit(solution)/shard_map/ppermute | solution.py:22
  63.9 27.8 %collective-permute-start.10 = (bf16[1,2,2,256,256]{4,3,2,1,0:T(8,128)(2,1)}, bf16[1,2,2,256,256]{4,3,2,1,0:T(8,128)(2,1)}, u32[]{:S(2)}, u32[]{:S(2)}) collective-permute-start(bf16[1,2,2,256,256]{4,3,2,1,0:T(8,128)(2,1)} %maximum_bitcast_fusion.1), channel_id=1, source_target_pairs={{0,6},{2,4},{4,2},{6,0},{1,7},{3,5},{5,3},{7,1},{8,14},{10,12},{12... | collective-permute-start | bytes 1572872 | tf_op jit(solution)/shard_map/ppermute | solution.py:22
  91.8 15.9 %collective-permute-start.13 = (bf16[400,2048]{1,0:T(8,128)(2,1)S(1)}, bf16[400,2048]{1,0:T(8,128)(2,1)}, u32[]{:S(2)}, u32[]{:S(2)}) collective-permute-start(bf16[400,2048]{1,0:T(8,128)(2,1)S(1)} %pad_maximum_fusion.1), channel_id=1, source_target_pairs={{0,8},{8,0},{1,9},{9,1},{2,10},{10,2},{3,11},{11,3},{4,12},{12,4},... | collective-permute-start | bytes 4915208 | tf_op jit(solution)/shard_map/ppermute | solution.py:22
  91.9 15.8 %collective-permute-start.12 = (bf16[144,2048]{1,0:T(8,128)(2,1)S(1)}, bf16[144,2048]{1,0:T(8,128)(2,1)}, u32[]{:S(2)}, u32[]{:S(2)}) collective-permute-start(bf16[144,2048]{1,0:T(8,128)(2,1)S(1)} %pad_maximum_fusion.5.refs_5_), channel_id=1, source_target_pairs={{0,1},{1,0},{2,3},{3,2},{4,5},{5,4},{6,7},{7,6},{8,9},{9,8},{10,11... | collective-permute-start | bytes 1769480 | tf_op jit(solution)/shard_map/ppermute | solution.py:22
  92.5 15.0 %collective-permute-start.14 = (bf16[1,2,2,256,256]{4,3,2,1,0:T(8,128)(2,1)}, bf16[1,2,2,256,256]{4,3,2,1,0:T(8,128)(2,1)S(1)}, u32[]{:S(2)}, u32[]{:S(2)}) collective-permute-start(bf16[1,2,2,256,256]{4,3,2,1,0:T(8,128)(2,1)} %collective-permute-done.10.refs_14_), channel_id=1, source_target_pairs={{0,16},{16,0},{1,17},{17,1},{2,18},{18,2},{3,19},{19,3},{4,20},{20... | collective-permute-start | bytes 1572872 | tf_op jit(solution)/shard_map/ppermute | solution.py:22
  92.9 14.6 %collective-permute-start.15 = (bf16[1,2,1,256,256]{4,3,2,1,0:T(8,128)(2,1)S(1)}, bf16[1,2,1,256,256]{4,3,2,1,0:T(8,128)(2,1)S(1)}, u32[]{:S(2)}, u32[]{:S(2)}) collective-permute-start(bf16[1,2,1,256,256]{4,3,2,1,0:T(8,128)(2,1)S(1)} %maximum_bitcast_fusion.2.refs_11_), channel_id=1, source_target_pairs={{0,4},{2,6},{4,0},{6,2},{1,5},{3,7},{5,1},{7,3},{8,12},{10,14},{12... | collective-permute-start | bytes 786440 | tf_op jit(solution)/shard_map/ppermute | solution.py:22
  94.9 12.6 %collective-permute-start.16 = (bf16[1,2,1,256,256]{4,3,2,1,0:T(8,128)(2,1)S(1)}, bf16[1,2,1,256,256]{4,3,2,1,0:T(8,128)(2,1)S(1)}, u32[]{:S(2)}, u32[]{:S(2)}) collective-permute-start(bf16[1,2,1,256,256]{4,3,2,1,0:T(8,128)(2,1)S(1)} %copy-done.12), channel_id=1, source_target_pairs={{0,2},{2,0},{4,6},{6,4},{1,3},{3,1},{5,7},{7,5},{8,10},{10,8},{12,... | collective-permute-start | bytes 786440 | tf_op jit(solution)/shard_map/ppermute | solution.py:22
  110.7 14.7 %collective-permute-start.18 = (bf16[1,2,1,256,256]{4,3,2,1,0:T(8,128)(2,1)}, bf16[1,2,1,256,256]{4,3,2,1,0:T(8,128)(2,1)S(1)}, u32[]{:S(2)}, u32[]{:S(2)}) collective-permute-start(bf16[1,2,1,256,256]{4,3,2,1,0:T(8,128)(2,1)} %maximum_bitcast_fusion.3), channel_id=1, source_target_pairs={{0,6},{2,4},{4,2},{6,0},{1,7},{3,5},{5,3},{7,1},{8,14},{10,12},{12... | collective-permute-start | bytes 786440 | tf_op jit(solution)/shard_map/ppermute | solution.py:22
  113.1 13.8 %collective-permute-start.19 = (bf16[2,2,1,256,256]{4,3,2,1,0:T(8,128)(2,1)S(1)}, bf16[2,2,1,256,256]{4,3,2,1,0:T(8,128)(2,1)}, u32[]{:S(2)}, u32[]{:S(2)}) collective-permute-start(bf16[2,2,1,256,256]{4,3,2,1,0:T(8,128)(2,1)S(1)} %pad_maximum_fusion.6), channel_id=1, source_target_pairs={{0,16},{16,0},{1,17},{17,1},{2,18},{18,2},{3,19},{19,3},{4,20},{20... | collective-permute-start | bytes 1572872 | tf_op jit(solution)/shard_map/ppermute | solution.py:22
  126.9 10.9 %collective-permute-start.20 = (bf16[4,64,256]{2,1,0:T(8,128)(2,1)}, bf16[4,64,256]{2,1,0:T(8,128)(2,1)S(1)}, u32[]{:S(2)}, u32[]{:S(2)}) collective-permute-start(bf16[4,64,256]{2,1,0:T(8,128)(2,1)} %get-tuple-element.58), channel_id=1, source_target_pairs={{0,4},{4,0},{16,20},{20,16},{1,5},{5,1},{17,21},{21,17},{2,6},{6,2... | collective-permute-start | bytes 393224 | tf_op jit(solution)/shard_map/ppermute | solution.py:22
  127.0 10.8 %collective-permute-start.21 = (bf16[4,64,256]{2,1,0:T(8,128)(2,1)}, bf16[4,64,256]{2,1,0:T(8,128)(2,1)S(1)}, u32[]{:S(2)}, u32[]{:S(2)}) collective-permute-start(bf16[4,64,256]{2,1,0:T(8,128)(2,1)} %get-tuple-element.59), channel_id=1, source_target_pairs={{0,16},{4,20},{16,0},{20,4},{1,17},{5,21},{17,1},{21,5},{2,18},{6,... | collective-permute-start | bytes 393224 | tf_op jit(solution)/shard_map/ppermute | solution.py:22
  127.4 12.9 %collective-permute-start.22 = (bf16[4,64,256]{2,1,0:T(8,128)(2,1)}, bf16[4,64,256]{2,1,0:T(8,128)(2,1)S(1)}, u32[]{:S(2)}, u32[]{:S(2)}) collective-permute-start(bf16[4,64,256]{2,1,0:T(8,128)(2,1)} %get-tuple-element.60), channel_id=1, source_target_pairs={{0,20},{4,16},{16,4},{20,0},{1,21},{5,17},{17,5},{21,1},{2,22},{6,... | collective-permute-start | bytes 393224 | tf_op jit(solution)/shard_map/ppermute | solution.py:22
  140.3 16.9 %collective-permute-start.23 = (bf16[2,2,1,256,256]{4,3,2,1,0:T(8,128)(2,1)S(1)}, bf16[2,2,1,256,256]{4,3,2,1,0:T(8,128)(2,1)S(1)}, u32[]{:S(2)}, u32[]{:S(2)}) collective-permute-start(bf16[2,2,1,256,256]{4,3,2,1,0:T(8,128)(2,1)S(1)} %pad_maximum_fusion.7), channel_id=1, source_target_pairs={{0,16},{16,0},{1,17},{17,1},{2,18},{18,2},{3,19},{19,3},{4,20},{20... | collective-permute-start | bytes 1572872 | tf_op jit(solution)/shard_map/ppermute | solution.py:22
  157.2 22.5 %all-to-all-start.1 = ((bf16[16,64,256]{2,1,0:T(8,128)(2,1)}), bf16[16,64,256]{2,1,0:T(8,128)(2,1)S(1)}, u32[]{:S(2)}, u32[]{:S(2)}) async-start(bf16[16,64,256]{2,1,0:T(8,128)(2,1)} %long_conv.1), calls=%async_computation.1 | async-start | bytes 1048576 | tf_op jit(solution)/shard_map/all_to_all | solution.py:442
  (27 other events, 319.6 us)
